TPU v7x, 256 devices: a whole 4x4x8 slice. The times are simulated.
256 devices in a mesh: tile: 32 (over y, z), grp: 8 (over x, core).
Axes of the slice: x: 4, y: 4, z: 8, core: 2. Of those that a mesh axis runs over, the one named last changes fastest.
Arguments:
- state: bfloat16 [512, 1024, 556], P('tile', 'grp'), may hold values from -6 to 6
- courant: bfloat16 [512, 1024, 2], P('tile', 'grp'), may hold values from -0.44921875 to 0.44921875
- route: int32 [32, 8, 2048, 1], P('tile', 'grp'), may hold values from 0 to 31; in each aligned block of 2048 rows (0 to 2047, 2048 to 4095, ..., all dimensions but the last counted through in order) at most 96 rows name the same one
- counts: int32 [512], P('tile'), may hold values from 128 to 1024, as said below
- w_in: bfloat16 [32, 556, 512], P('tile'), may hold values from -0.25 to 0.25
- w_mid: bfloat16 [32, 3, 512, 512], P('tile'), may hold values from -0.375 to 0.375
- w_out: bfloat16 [32, 512, 368], P('tile'), may hold values from -0.375 to 0.375
Outputs:
- advected: bfloat16 [512, 1024, 556], P('tile', 'grp')
- tendency: bfloat16 [512, 1024, 368], P('tile', 'grp')
Inputs may be any that keep to these rules, and one draw needn't show every extreme that they name: `route`: each column names one expert; at most 96 columns of one device name the same expert, and some expert reaches it. `counts`: rows of the middle half of latitudes are full.
All inputs are finite; a program needn't handle non-finite values.
Results may differ from a plain program's by a relative error of at most 0.008.
Values may be sent and summed in bfloat16 or wider, within the bound.
A program may use at most 128 MiB of HBM per device.

v0:
```python
import jax
import jax.numpy as jnp
from jax import lax
from jax.sharding import PartitionSpec as P

STEPS = 2


def extended(cells, sides, width, closed):
    for axis, dim in sides:
        count = lax.axis_size(axis)
        ends = count if closed else count - 1
        head = lax.slice_in_dim(cells, 0, width, axis=dim)
        tail = lax.slice_in_dim(cells, cells.shape[dim] - width, cells.shape[dim], axis=dim)
        cells = jnp.concatenate(
            [
                lax.ppermute(tail, axis, [(i, (i + 1) % count) for i in range(ends)]),
                cells,
                lax.ppermute(head, axis, [((i + 1) % count, i) for i in range(ends)]),
            ],
            axis=dim,
        )
    return cells


def advance(q, cour):
    centre = q[1:-1, 1:-1]
    north = q[2:, 1:-1]
    south = q[:-2, 1:-1]
    east = q[1:-1, 2:]
    west = q[1:-1, :-2]
    u = cour[1:-1, 1:-1, 0:1]
    v = cour[1:-1, 1:-1, 1:2]
    return (
        centre
        - (jnp.maximum(u, 0.0) * (centre - west) + jnp.minimum(u, 0.0) * (east - centre))
        - (jnp.maximum(v, 0.0) * (centre - south) + jnp.minimum(v, 0.0) * (north - centre))
    )


def apply_net(rows, first, middle, last):
    hidden = jax.nn.leaky_relu(
        jnp.dot(rows, first, preferred_element_type=jnp.float32), 0.15
    ).astype(jnp.bfloat16)
    for layer in range(middle.shape[0]):
        hidden = jax.nn.leaky_relu(
            jnp.dot(hidden, middle[layer], preferred_element_type=jnp.float32), 0.15
        ).astype(jnp.bfloat16)
    return jnp.dot(hidden, last, preferred_element_type=jnp.float32).astype(jnp.bfloat16)


def on_device(state, courant, route, counts, w_in, w_mid, w_out):
    lat_dev, lon_dev, feats = state.shape
    advected = state
    for step in range(STEPS):
        packed = jnp.concatenate([advected, courant], axis=2)
        wide = extended(packed, (("grp", 1),), 1, True)
        wide = extended(wide, (("tile", 0),), 1, False)
        q_now = wide[:, :, :feats].astype(jnp.float32)
        cour = wide[:, :, feats:].astype(jnp.float32)
        advected = advance(q_now, cour).astype(jnp.bfloat16)
    columns = lat_dev * lon_dev
    members = lax.axis_size("tile")
    cap = max(2, (3 * columns + 2 * members - 1) // (2 * members))
    lon_global = lax.axis_index("grp") * lon_dev + jnp.arange(lon_dev, dtype=jnp.int32)
    active = (lon_global[None, :] < counts[:, None]).reshape(columns)
    flat_cols = advected.reshape(columns, feats)
    inputs = jnp.where(active[:, None], flat_cols, jnp.zeros_like(flat_cols))
    member = route.reshape(columns)
    onehot = (member[:, None] == jnp.arange(members, dtype=jnp.int32)[None, :]).astype(jnp.int32)
    slot = jnp.sum((jnp.cumsum(onehot, axis=0) - 1) * onehot, axis=1)
    place = member * cap + slot
    outgoing = (
        jnp.zeros((members * cap, feats), jnp.bfloat16)
        .at[place]
        .set(inputs)
        .reshape(members, cap, feats)
    )
    first = w_in[0]
    middle = w_mid[0]
    last = w_out[0]
    received = lax.all_to_all(outgoing, "tile", split_axis=0, concat_axis=0, tiled=True)
    result = apply_net(received.reshape(members * cap, feats), first, middle, last)
    result = result.reshape(members, cap, result.shape[-1])
    returned = lax.all_to_all(result, "tile", split_axis=0, concat_axis=0, tiled=True)
    returned = returned.reshape(members * cap, returned.shape[-1])
    tend = returned[place]
    tend = jnp.where(active[:, None], tend, jnp.zeros_like(tend))
    return (advected, tend.reshape(lat_dev, lon_dev, tend.shape[-1]))


def solution(mesh):
    in_specs = (
        P("tile", "grp", None),
        P("tile", "grp", None),
        P("tile", "grp", None, None),
        P("tile"),
        P("tile", None, None),
        P("tile", None, None, None),
        P("tile", None, None),
    )
    out_specs = (P("tile", "grp", None), P("tile", "grp", None))
    return jax.shard_map(
        on_device, mesh=mesh, in_specs=in_specs, out_specs=out_specs, check_vma=False
    )
```

profile of v0, /device:TPU:6, one launch (start us, length us, event | category | flops | bytes accessed | tf_op | source)
XLA Modules:
  0.0 392.6 jit_solution(11257262742695116838)
XLA Ops:
  0.7 2.1 constant_dynamic-update-slice_fusion.1
  2.8 3.1 fusion.80
  5.9 2.7 copy.61
  8.6 2.7 copy.62
  11.3 1.7 collective-permute-start.1
  13.1 9.1 %reduce-window.6 = s32[32,16,128]{2,1,0:T(8,128)S(1)} reduce-window(s32[32,16,128]{2,1,0:T(8,128)S(1)} %fusion.62, s32[]{:T(128)} %constant.15.clone.1), window={size=1x1x128 pad=0_0x0_0x127_0}, to_apply=%region_0.1 | reduce-window | flops 8323072 | bytes 524292 | tf_op jit(solution)/shard_map/reduce-window
  22.2 0.1 slice.145
  22.3 0.2 copy.83
  22.6 0.2 reduce-window.9
  22.8 0.1 add_add_fusion
  22.9 0.1 fusion.61
  23.0 2.6 copy.63
  25.7 2.6 copy.64
  28.3 6.0 %pad_maximum_fusion.9 = (bf16[1,130,558]{1,0,2:T(2,128)(2,1)}, bf16[1,130,558]{1,0,2:T(2,128)(2,1)S(1)}) fusion(bf16[16,1,558]{1,0,2:T(8,128)(2,1)} %copy.64, bf16[16,128,558]{1,0,2:T(8,128)(2,1)S(1)} %get-tuple-element.26, bf16[16,1,558]{1,0,2:T(8,128)(2,1)} %copy.63), kind=kLoop, calls=%fused_computation.66 | loop fusion | flops 870480 | bytes 2611440 | tf_op jit(solution)/shard_map/slice | solution.py:14
  34.3 1.9 copy.65
  36.2 4.5 %collective-permute-start.2 = (bf16[1,130,558]{2,1,0:T(8,128)(2,1)}, bf16[1,130,558]{2,1,0:T(8,128)(2,1)}, u32[]{:S(2)}, u32[]{:S(2)}) collective-permute-start(bf16[1,130,558]{2,1,0:T(8,128)(2,1)} %copy.65), channel_id=1, source_target_pairs={{0,8},{8,16},{16,24},{24,32},{32,40},{40,48},{48,56},{56,64},{64,7... | collective-permute-start | bytes 435248 | tf_op jit(solution)/shard_map/ppermute | solution.py:17
  40.6 1.4 copy.66
  42.0 1.7 collective-permute-start.3
  43.8 1.7 copy.67
  45.5 4.1 %collective-permute-done.3 = bf16[1,130,558]{2,1,0:T(8,128)(2,1)} collective-permute-done((bf16[1,130,558]{2,1,0:T(8,128)(2,1)}, bf16[1,130,558]{2,1,0:T(8,128)(2,1)}, u32[]{:S(2)}, u32[]{:S(2)}) %collective-permute-start.3) | collective-permute-done | bytes 145112 | tf_op jit(solution)/shard_map/ppermute | solution.py:19
  49.6 2.1 copy.68
  51.7 0.9 fusion.67
  52.6 0.7 copy-done.1
  53.3 0.7 copy-done.2
  54.0 0.1 copy-done.6
  54.1 8.2 %pad_maximum_fusion = bf16[18,130,558]{1,0,2:T(8,128)(2,1)S(1)} fusion(bf16[1,130,558]{1,0,2:T(2,128)(2,1)S(1)} %copy-done.6, bf16[16,1,558]{1,0,2:T(8,128)(2,1)S(1)} %copy-done.2, bf16[16,128,558]{1,0,2:T(8,128)(2,1)S(1)} %get-tuple-element.26, bf16[16,1,558]{1,0,2:T(8,128)(2,1)S(1)} %copy-done.1, bf16[1,130,558]{1,0,2:T(2,128)(2,1)S(1)} %copy.67), kind=kLoop, calls=%fused_computation.6 | loop fusion | flops 13057200 | bytes 5222880 | tf_op jit(solution)/shard_map/concatenate | solution.py:15
  62.4 6.0 %slice_convert_fusion.1 = f32[18,130,556]{1,0,2:T(8,128)} fusion(bf16[18,130,558]{1,0,2:T(8,128)(2,1)S(1)} %pad_maximum_fusion), kind=kLoop, calls=%fused_computation.9 | loop fusion | flops 1301040 | bytes 7806240 | tf_op jit(solution)/shard_map/convert_element_type | solution.py:59
  68.4 22.2 %fusion.16 = bf16[16,128,556]{1,0,2:T(8,128)(2,1)S(1)} fusion(f32[18,130,556]{1,0,2:T(8,128)} %slice_convert_fusion.1, f32[16,128]{1,0:T(8,128)S(1)} %get-tuple-element.30, f32[16,128]{1,0:T(8,128)S(1)} %get-tuple-element.16, f32[16,128]{1,0:T(8,128)S(1)} %get-tuple-element.31, f32[16,128]{1,0:T(8,128)S(1)} %get-tuple-element.10), kind=kLoop, calls=%fused_computation.31 | loop fusion | flops 14802944 | bytes 25083904 | tf_op jit(solution)/shard_map/convert_element_type | solution.py:61
  90.6 3.0 slice_maximum_fusion
  93.7 2.7 copy.70
  96.4 2.7 copy.71
  99.1 1.7 collective-permute-start.5
  100.8 2.6 copy.72
  103.5 2.6 copy.73
  106.1 7.8 %pad_maximum_fusion.6 = (bf16[1,130,558]{1,0,2:T(2,128)(2,1)}, bf16[1,130,558]{1,0,2:T(2,128)(2,1)S(1)}) fusion(bf16[16,1,558]{1,0,2:T(8,128)(2,1)} %copy.73, bf16[16,1,558]{1,0,2:T(8,128)(2,1)} %copy.72, bf16[16,128,2]{1,0,2:T(8,128)(2,1)S(1)} %get-tuple-element.27, bf16[16,128,556]{1,0,2:T(8,128)(2,1)S(1)} %fusion.16), kind=kLoop, calls=%fused_computation.63 | loop fusion | flops 1160640 | bytes 2611440 | tf_op jit(solution)/shard_map/slice | solution.py:14
  113.8 1.9 copy.74
  115.7 3.8 collective-permute-start.6
  119.6 1.4 copy.75
  120.9 1.3 collective-permute-start.7
  122.2 0.1 broadcast_compare_fusion
  122.3 0.9 collective-permute-done.6
  123.2 1.8 copy.76
  125.0 4.9 %collective-permute-done.7 = bf16[1,130,558]{2,1,0:T(8,128)(2,1)} collective-permute-done((bf16[1,130,558]{2,1,0:T(8,128)(2,1)}, bf16[1,130,558]{2,1,0:T(8,128)(2,1)}, u32[]{:S(2)}, u32[]{:S(2)}) %collective-permute-start.7) | collective-permute-done | bytes 145112 | tf_op jit(solution)/shard_map/ppermute | solution.py:19
  129.9 2.1 copy.77
  132.0 0.9 fusion.69
  132.9 0.7 copy-done.3
  133.6 0.7 copy-done.4
  134.3 0.1 copy-done.5
  134.4 12.2 %pad_maximum_fusion.1 = bf16[18,130,558]{1,0,2:T(8,128)(2,1)S(1)} fusion(bf16[1,130,558]{1,0,2:T(2,128)(2,1)S(1)} %copy-done.5, bf16[16,1,558]{1,0,2:T(8,128)(2,1)S(1)} %copy-done.4, bf16[16,128,2]{1,0,2:T(8,128)(2,1)S(1)} %get-tuple-element.27, bf16[16,128,556]{1,0,2:T(8,128)(2,1)S(1)} %fusion.16, bf16[16,1,558]{1,0,2:T(8,128)(2,1)S(1)} %copy-done.3, ...), kind=kLoop, calls=%fused_computation.7 | loop fusion | flops 15668640 | bytes 5222880 | tf_op jit(solution)/shard_map/concatenate | solution.py:15
  146.6 6.0 %slice_convert_fusion = f32[18,130,556]{1,0,2:T(8,128)} fusion(bf16[18,130,558]{1,0,2:T(8,128)(2,1)S(1)} %pad_maximum_fusion.1), kind=kLoop, calls=%fused_computation.8 | loop fusion | flops 1301040 | bytes 7806240 | tf_op jit(solution)/shard_map/convert_element_type | solution.py:59
  152.7 23.2 %fusion.7 = bf16[16,128,556]{1,0,2:T(8,128)(2,1)} fusion(f32[18,130,556]{1,0,2:T(8,128)} %slice_convert_fusion, f32[16,128]{1,0:T(8,128)S(1)} %fusion.65, f32[16,128]{1,0:T(8,128)S(1)} %get-tuple-element.14, f32[16,128]{1,0:T(8,128)S(1)} %fusion.70, f32[16,128]{1,0:T(8,128)S(1)} %get-tuple-element.6), kind=kLoop, calls=%fused_computation.18 | loop fusion | flops 14802944 | bytes 25083904 | tf_op jit(solution)/shard_map/convert_element_type | solution.py:61
  175.8 3.8 copy.84
  179.6 2.1 bitcast_select_fusion
  181.7 12.7 %scatter_custom_fusion = bf16[3072,556]{1,0:T(8,128)(2,1)} fusion(s32[2048]{0:T(1024)S(1)} %bitcast.78, bf16[2048,556]{1,0:T(8,128)(2,1)} %bitcast_select_fusion, bf16[]{:T(256)} %constant.12.clone.1), kind=kCustom, calls=%fused_computation.55 | custom fusion | bytes 3416576 | tf_op jit(solution)/shard_map/scatter | solution.py:76
  194.4 100.2 %all_to_all.10 = bf16[32,96,556]{2,1,0:T(8,128)(2,1)S(1)} all-to-all(bf16[32,96,556]{2,1,0:T(8,128)(2,1)} %bitcast.68), channel_id=1, replica_groups=mesh['tile'=32,'grp'=8] {'tile'}, dimensions={0} | all-to-all | bytes 6832128 | tf_op jit(solution)/shard_map/all_to_all | solution.py:82
  294.7 4.5 %fusion.47 = f32[3072,512]{1,0:T(8,128)} fusion(bf16[3072,556]{1,0:T(8,128)(2,1)S(1)} %bitcast.71, bf16[1,556,512]{2,1,0:T(8,128)(2,1)S(1)} %copy-done), kind=kOutput, calls=%fused_computation.58 | convolution fusion | flops 1749024768 | bytes 10276864 | tf_op jit(solution)/shard_map/dot_general | solution.py:43
  299.2 9.0 %fusion.25 = f32[3072,512]{1,0:T(8,128)} fusion(f32[3072,512]{1,0:T(8,128)} %fusion.47, bf16[1,3,512,512]{3,2,1,0:T(8,128)(2,1)S(1)} %copy-done.10), kind=kOutput, calls=%fused_computation.42 | convolution fusion | flops 3233808384 | bytes 13631488 | tf_op jit(solution)/shard_map/dot_general | solution.py:47
  308.1 6.0 %convolution_convert_fusion = bf16[3072,368]{0,1:T(8,128)(2,1)S(1)} fusion(f32[3072,512]{1,0:T(8,128)} %fusion.25, bf16[1,3,512,512]{3,2,1,0:T(8,128)(2,1)} %param.12, bf16[1,512,368]{1,2,0:T(8,128)(2,1)S(1)} %copy-done.11), kind=kOutput, calls=%fused_computation.40 | convolution fusion | flops 2781954048 | bytes 9453568 | tf_op jit(solution)/shard_map/dot_general | solution.py:49
  314.1 2.4 copy.81
  316.5 5.8 %all-to-all-start.1 = ((bf16[32,96,368]{2,1,0:T(8,128)(2,1)}), bf16[32,96,368]{2,1,0:T(8,128)(2,1)S(1)}, u32[]{:S(2)}, u32[]{:S(2)}) async-start(bf16[32,96,368]{2,1,0:T(8,128)(2,1)} %bitcast.69), calls=%async_computation.1 | async-start | bytes 4718592 | tf_op jit(solution)/shard_map/all_to_all | solution.py:85
  322.3 57.8 %all-to-all-done.1 = bf16[32,96,368]{2,1,0:T(8,128)(2,1)S(1)} async-done(((bf16[32,96,368]{2,1,0:T(8,128)(2,1)}), bf16[32,96,368]{2,1,0:T(8,128)(2,1)S(1)}, u32[]{:S(2)}, u32[]{:S(2)}) %all-to-all-start.1) | async-done | bytes 2261024 | tf_op jit(solution)/shard_map/all_to_all | solution.py:85
  380.1 9.1 %gather_fusion = bf16[2048,368]{1,0:T(8,128)(2,1)} fusion(bf16[3072,368]{1,0:T(8,128)(2,1)S(1)} %bitcast.67, s32[2048]{0:T(1024)S(1)} %broadcast_clamp_fusion), kind=kCustom, calls=%fused_computation | custom fusion | bytes 3022848 | tf_op jit(solution)/shard_map/gather | solution.py:87
  389.2 1.9 copy.82
  391.1 1.2 broadcast_select_fusion
  (33 shorter events, 0.2 us)
Async XLA Ops:
  0.6 294.0 %copy-start = (bf16[1,556,512]{2,1,0:T(8,128)(2,1)S(1)}, bf16[1,556,512]{2,1,0:T(8,128)(2,1)}, u32[]{:S(2)}) copy-start(bf16[1,556,512]{2,1,0:T(8,128)(2,1)} %param.11) | copy-start | bytes 1708036
  0.6 2.1 copy-start.8
  5.9 7.2 %copy-start.7 = (s32[1,1,2048,1]{2,3,1,0:T(1,128)S(1)}, s32[1,1,2048,1]{2,3,1,0:T(1,128)}, u32[]{:S(2)}) copy-start(s32[1,1,2048,1]{2,3,1,0:T(1,128)} %param.9) | copy-start | bytes 24580
  8.6 14.4 %collective-permute-start = (bf16[16,1,558]{2,0,1:T(8,128)(2,1)S(1)}, bf16[16,1,558]{2,0,1:T(8,128)(2,1)S(1)}, u32[]{:S(2)}, u32[]{:S(2)}) collective-permute-start(bf16[16,1,558]{2,0,1:T(8,128)(2,1)S(1)} %copy.61), channel_id=1, source_target_pairs={{0,1},{1,2},{2,3},{3,4},{4,5},{5,6},{6,7},{7,0},{8,9},{9,10},{10,1... | collective-permute-start | bytes 53576 | tf_op jit(solution)/shard_map/ppermute | solution.py:17
  11.3 14.3 %collective-permute-start.1 = (bf16[16,1,558]{2,0,1:T(8,128)(2,1)S(1)}, bf16[16,1,558]{2,0,1:T(8,128)(2,1)S(1)}, u32[]{:S(2)}, u32[]{:S(2)}) collective-permute-start(bf16[16,1,558]{2,0,1:T(8,128)(2,1)S(1)} %copy.62), channel_id=1, source_target_pairs={{1,0},{2,1},{3,2},{4,3},{5,4},{6,5},{7,6},{0,7},{9,8},{10,9},{11,1... | collective-permute-start | bytes 53576 | tf_op jit(solution)/shard_map/ppermute | solution.py:19
  36.2 7.6 %collective-permute-start.2 = (bf16[1,130,558]{2,1,0:T(8,128)(2,1)}, bf16[1,130,558]{2,1,0:T(8,128)(2,1)}, u32[]{:S(2)}, u32[]{:S(2)}) collective-permute-start(bf16[1,130,558]{2,1,0:T(8,128)(2,1)} %copy.65), channel_id=1, source_target_pairs={{0,8},{8,16},{16,24},{24,32},{32,40},{40,48},{48,56},{56,64},{64,7... | collective-permute-start | bytes 435248 | tf_op jit(solution)/shard_map/ppermute | solution.py:17
  42.0 7.6 %collective-permute-start.3 = (bf16[1,130,558]{2,1,0:T(8,128)(2,1)}, bf16[1,130,558]{2,1,0:T(8,128)(2,1)}, u32[]{:S(2)}, u32[]{:S(2)}) collective-permute-start(bf16[1,130,558]{2,1,0:T(8,128)(2,1)} %copy.66), channel_id=1, source_target_pairs={{8,0},{16,8},{24,16},{32,24},{40,32},{48,40},{56,48},{64,56},{72,6... | collective-permute-start | bytes 435248 | tf_op jit(solution)/shard_map/ppermute | solution.py:19
  51.7 1.7 copy-start.1
  51.7 2.3 copy-start.2
  51.7 2.4 copy-start.6
  96.4 4.5 %collective-permute-start.4 = (bf16[16,1,558]{2,0,1:T(8,128)(2,1)S(1)}, bf16[16,1,558]{2,0,1:T(8,128)(2,1)S(1)}, u32[]{:S(2)}, u32[]{:S(2)}) collective-permute-start(bf16[16,1,558]{2,0,1:T(8,128)(2,1)S(1)} %copy.70), channel_id=1, source_target_pairs={{0,1},{1,2},{2,3},{3,4},{4,5},{5,6},{6,7},{7,0},{8,9},{9,10},{10,1... | collective-permute-start | bytes 53576 | tf_op jit(solution)/shard_map/ppermute | solution.py:17
  99.1 4.4 %collective-permute-start.5 = (bf16[16,1,558]{2,0,1:T(8,128)(2,1)S(1)}, bf16[16,1,558]{2,0,1:T(8,128)(2,1)S(1)}, u32[]{:S(2)}, u32[]{:S(2)}) collective-permute-start(bf16[16,1,558]{2,0,1:T(8,128)(2,1)S(1)} %copy.71), channel_id=1, source_target_pairs={{1,0},{2,1},{3,2},{4,3},{5,4},{6,5},{7,6},{0,7},{9,8},{10,9},{11,1... | collective-permute-start | bytes 53576 | tf_op jit(solution)/shard_map/ppermute | solution.py:19
  106.1 16.1 %copy-start.9 = (s32[16]{0:T(128)S(1)}, s32[16]{0:T(128)}, u32[]{:S(2)}) copy-start(s32[16]{0:T(128)} %param.10) | copy-start | bytes 196
  115.7 7.4 %collective-permute-start.6 = (bf16[1,130,558]{2,1,0:T(8,128)(2,1)}, bf16[1,130,558]{2,1,0:T(8,128)(2,1)}, u32[]{:S(2)}, u32[]{:S(2)}) collective-permute-start(bf16[1,130,558]{2,1,0:T(8,128)(2,1)} %copy.74), channel_id=1, source_target_pairs={{0,8},{8,16},{16,24},{24,32},{32,40},{40,48},{48,56},{56,64},{64,7... | collective-permute-start | bytes 435248 | tf_op jit(solution)/shard_map/ppermute | solution.py:17
  120.9 9.0 %collective-permute-start.7 = (bf16[1,130,558]{2,1,0:T(8,128)(2,1)}, bf16[1,130,558]{2,1,0:T(8,128)(2,1)}, u32[]{:S(2)}, u32[]{:S(2)}) collective-permute-start(bf16[1,130,558]{2,1,0:T(8,128)(2,1)} %copy.75), channel_id=1, source_target_pairs={{8,0},{16,8},{24,16},{32,24},{40,32},{48,40},{56,48},{64,56},{72,6... | collective-permute-start | bytes 435248 | tf_op jit(solution)/shard_map/ppermute | solution.py:19
  132.0 1.7 copy-start.3
  132.0 2.3 copy-start.4
  132.0 2.4 copy-start.5
  294.7 4.5 %copy-start.10 = (bf16[1,3,512,512]{3,2,1,0:T(8,128)(2,1)S(1)}, bf16[1,3,512,512]{3,2,1,0:T(8,128)(2,1)}, u32[]{:S(2)}) copy-start(bf16[1,3,512,512]{3,2,1,0:T(8,128)(2,1)} %param.12) | copy-start | bytes 4718596
  299.2 9.0 %copy-start.11 = (bf16[1,512,368]{1,2,0:T(8,128)(2,1)S(1)}, bf16[1,512,368]{1,2,0:T(8,128)(2,1)}, u32[]{:S(2)}) copy-start(bf16[1,512,368]{1,2,0:T(8,128)(2,1)} %param.13) | copy-start | bytes 1130500
  316.5 63.6 %all-to-all-start.1 = ((bf16[32,96,368]{2,1,0:T(8,128)(2,1)}), bf16[32,96,368]{2,1,0:T(8,128)(2,1)S(1)}, u32[]{:S(2)}, u32[]{:S(2)}) async-start(bf16[32,96,368]{2,1,0:T(8,128)(2,1)} %bitcast.69), calls=%async_computation.1 | async-start | bytes 4718592 | tf_op jit(solution)/shard_map/all_to_all | solution.py:85
where the time goes:
time: 399 us; the launch traced here: 393 us
  other arithmetic  109 us (27%)
  blocking collectives  100 us (25%)
  local copies, waits for them, and re-layouts  74 us (19%)
  waiting for transfers between devices  67.8 us (17%)
  starting transfers between devices  20.6 us (5%)
  matrix products  19.4 us (5%)
    all_to_all x1, blocking collectives, on_device(): lax.all_to_all(outgoing, 'tile', split_axis=0, concat_axis=0, tiled=True)  100 us
    all_to_all x1, waiting for transfers between devices, on_device(): lax.all_to_all(result, 'tile', split_axis=0, concat_axis=0, tiled=True)  57.8 us
    convert_element_type x2, other arithmetic, on_device(): advected = advance(q_now, cour).astype(jnp.bfloat16)  45.4 us
    concatenate x2, other arithmetic, extended(): jnp.concatenate([lax.ppermute(tail, axis, [(i, (i + 1) % count) for i in...  20.4 us
    slice x2, other arithmetic, extended(): lax.slice_in_dim(cells, cells.shape[dim] - width, cells.shape[dim], axis=...  13.8 us
    scatter x1, local copies, waits for them, and re-layouts, on_device(): outgoing = jnp.zeros((members * cap, feats), jnp.bfloat16).at[place].set(...  12.7 us
    slice x5, local copies, waits for them, and re-layouts, extended(): lax.slice_in_dim(cells, cells.shape[dim] - width, cells.shape[dim], axis=...  12.3 us
    convert_element_type x2, other arithmetic, on_device(): q_now = wide[:, :, :feats].astype(jnp.float32)  12 us
  transfers between devices with their start and end apart: 9, of which 4 were waited for; matrix products, arithmetic and copies ran while one was open for 7% of the time, Pallas kernels for 0%

commit v1 on v0

v1 whole, which is shorter than its diff:
```python
import jax
import jax.numpy as jnp
from jax import lax
from jax.experimental import pallas as pl
from jax.experimental.pallas import tpu as pltpu
from jax.sharding import PartitionSpec as P

BF = jnp.bfloat16
F32 = jnp.float32
MESH = pl.DeviceIdType.MESH

F, HID, OUTW, NMID = 556, 512, 368, 3
LAT, LON, COLS = 16, 128, 2048
CAP = 96
NEXP = 32
NTILE = 32
MAIN = 512
KIN = 576
ROWS_OUT = 4 * CAP + CAP // 2
ROWS_RET = 3 * CAP
W_MID = 4 * KIN
W_OUT = W_MID + NMID * 4 * HID
W_ROWS = W_OUT + 3 * HID
CHUNKS = 24
CH = W_ROWS // CHUNKS
LAG = 2
GB = 4
NG = NEXP // GB
LANES = [(0, 128), (128, 256), (256, 384), (384, 512), (512, F)]
ADV_POINTS = 7
POINTS = CHUNKS + 3 * LAG


def kernel(
    counts_ref, route_ref, state_hbm, cour_hbm, win_hbm, wmid_hbm, wout_hbm,
    adv_hbm, tend_ref,
    q0, q1, adv, xt, cour, ub, vb, nsh, ews, ewr, ewfs, ewfr, place, pcol, pmat,
    send, recv, rs, rr, wts, wi, wm, wo, xin,
    lsem, hs_sem, hr_sem, w_s1, w_s2, w_r, f_s, f_r, r_s, r_r,
):
    t = lax.axis_index("tile")
    g = lax.axis_index("grp")
    y, z, x, c = t // 8, t % 8, g // 2, g % 2

    def dest(k):
        j = lax.rem(k * 13, NEXP)
        return lax.rem(y + j // 8, 4), lax.rem(x + (j // 2) % 4, 4), lax.rem(c + j % 2, 2)

    def dest_id(k):
        ty, tx, tc = dest(k)
        return {"tile": ty * 8 + z, "grp": tx * 2 + tc}

    def dest_base(k):
        ty, tx, tc = dest(k)
        return (ty * 8 + tx + 4 * tc) * CAP

    def source_id(k):
        j = lax.rem(k * 13, NEXP)
        ty = lax.rem(y + 4 - j // 8, 4)
        tx = lax.rem(x + 4 - (j // 2) % 4, 4)
        return {"tile": ty * 8 + z, "grp": tx * 2 + lax.rem(c + j % 2, 2)}

    def ring_id(d):
        return {"tile": y * 8 + lax.rem(z + d + 8, 8)}

    def tile_id(d):
        return {"tile": lax.rem(t + d + NTILE, NTILE)}

    def grp_id(d):
        return {"grp": lax.rem(g + d + 8, 8)}

    rel = lax.rem(z + 8 - (x + 4 * c), 8)
    forward_up = (rel >= 1) & (rel <= 3)
    forward_down = rel >= 6
    hop = jnp.where(rel <= 4, rel, 8 - rel)

    cp_state = pltpu.make_async_copy(state_hbm, q0, lsem.at[0])
    cp_cour = pltpu.make_async_copy(cour_hbm, cour, lsem.at[1])
    cp_wi = pltpu.make_async_copy(win_hbm, wi, lsem.at[2])
    cp_wm = pltpu.make_async_copy(wmid_hbm, wm, lsem.at[3])
    cp_wo = pltpu.make_async_copy(wout_hbm, wo, lsem.at[4])
    cp_adv = pltpu.make_async_copy(adv, adv_hbm, lsem.at[5])
    cp_state.start()
    cp_cour.start()

    @pl.when(rel == 0)
    def _():
        cp_wi.start()
        cp_wm.start()
        cp_wo.start()

    barrier = pltpu.get_barrier_semaphore()

    def greet(k, carry):
        pl.semaphore_signal(barrier, inc=1, device_id=dest_id(k), device_id_type=MESH)
        return carry

    lax.fori_loop(1, NEXP, greet, 0)
    for d in (1, -1):
        pl.semaphore_signal(barrier, inc=1, device_id=ring_id(d), device_id_type=MESH)
        pl.semaphore_signal(barrier, inc=1, device_id=tile_id(d), device_id_type=MESH)
        pl.semaphore_signal(barrier, inc=1, device_id=grp_id(d), device_id_type=MESH)

    def halo(n, src, dst, device):
        return pltpu.make_async_remote_copy(
            src, dst, hs_sem.at[n], hr_sem.at[n], device_id=device, device_id_type=MESH
        )

    def halos(step, q):
        b = 4 * step
        return [
            halo(b, q.at[0], nsh.at[2 * step], tile_id(-1)),
            halo(b + 1, q.at[LAT - 1], nsh.at[2 * step + 1], tile_id(1)),
            halo(b + 2, ews.at[2 * step], ewr.at[2 * step], grp_id(-1)),
            halo(b + 3, ews.at[2 * step + 1], ewr.at[2 * step + 1], grp_id(1)),
        ]

    halo0, halo1 = halos(0, q0), halos(1, q1)

    def wcopy(k, d, sem):
        part = wts.at[pl.ds(pl.multiple_of(k * CH, CH), CH)]
        return pltpu.make_async_remote_copy(
            part, part, sem.at[k], w_r.at[k], device_id=ring_id(d), device_id_type=MESH
        )

    def ring_point(p):
        k = p - LAG * hop
        ok = (k >= 0) & (k < CHUNKS)

        @pl.when(ok & (rel == 0))
        def _():
            wcopy(k, 1, w_s1).start()
            wcopy(k, -1, w_s2).start()

        @pl.when(ok & forward_up)
        def _():
            wcopy(k, 1, w_s1).wait_recv()
            wcopy(k, 1, w_s1).start()

        @pl.when(ok & forward_down)
        def _():
            wcopy(k, -1, w_s1).wait_recv()
            wcopy(k, -1, w_s1).start()

    def ring_points(a, b):
        def one(p, carry):
            ring_point(p)
            return carry

        lax.fori_loop(a, b, one, 0)

    edge_no = lax.broadcasted_iota(jnp.int32, (LAT, 128), 0)

    def put_edge(n, i, a, b, row):
        ewfs[n, :, a:b] = jnp.where(edge_no[:, : b - a] == i, row, ewfs[n, :, a:b])

    def edges_of(i, carry):
        for a, b in LANES:
            put_edge(0, i, a, b, q0[i, 0:16, a:b].astype(F32)[0:1])
            put_edge(1, i, a, b, q0[i, LON - 16 : LON, a:b].astype(F32)[15:16])
        return carry

    cp_state.wait()
    lax.fori_loop(0, LAT, edges_of, 0)
    ews[0] = ewfs[0].astype(BF)
    ews[1] = ewfs[1].astype(BF)

    @pl.when(rel == 0)
    def _():
        cp_wi.wait()
        cp_wm.wait()
        cp_wo.wait()
        for n in range(4):
            wts[n * KIN + 544 : (n + 1) * KIN, :] = jnp.zeros((KIN - 544, 128), BF)
            wts[n * KIN : n * KIN + F, :] = wi[0, :, n * 128 : (n + 1) * 128]
        for k in range(NMID):
            for n in range(4):
                r = W_MID + (k * 4 + n) * HID
                wts[r : r + HID, :] = wm[0, k, :, n * 128 : (n + 1) * 128]
        for n in range(2):
            r = W_OUT + n * HID
            wts[r : r + HID, :] = wo[0, :, n * 128 : (n + 1) * 128]
        r = W_OUT + 2 * HID
        wts[r : r + HID, :] = jnp.zeros((HID, 128), BF)
        wts[r : r + HID, 0 : OUTW - 256] = wo[0, :, 256:OUTW]

    pl.semaphore_wait(barrier, NEXP - 1 + 6)
    for h in (halo0[2], halo0[3], halo0[0], halo0[1]):
        h.start()

    cp_cour.wait()

    def spread(i, carry):
        both = cour[i].astype(F32)
        ub[i] = jnp.broadcast_to(both[:, 0:1], (LON, 128))
        vb[i] = jnp.broadcast_to(both[:, 1:2], (LON, 128))
        return carry

    lax.fori_loop(0, LAT, spread, 0)

    lat_no = lax.broadcasted_iota(jnp.int32, (LAT, LON), 0)
    lon_no = lax.broadcasted_iota(jnp.int32, (LAT, LON), 1) + g * LON
    reach = jnp.zeros((LAT, LON), jnp.int32)
    for i in range(LAT):
        reach = jnp.where(lat_no == i, counts_ref[i], reach)
    member = jnp.where(lon_no < reach, route_ref[...], -1)
    named = jnp.concatenate([(member == m).astype(F32) for m in range(NEXP)], axis=0).astype(BF)
    before = (
        lax.broadcasted_iota(jnp.int32, (LON, LON), 0)
        < lax.broadcasted_iota(jnp.int32, (LON, LON), 1)
    )
    within = jnp.dot(named, before.astype(F32).astype(BF), preferred_element_type=F32)
    whole = jnp.dot(named, jnp.ones((LON, LON), BF), preferred_element_type=F32).astype(BF)
    r0 = lax.broadcasted_iota(jnp.int32, (NEXP * LAT, NEXP * LAT), 0)
    r1 = lax.broadcasted_iota(jnp.int32, (NEXP * LAT, NEXP * LAT), 1)
    rows_before = ((r0 // LAT == r1 // LAT) & (r1 < r0)).astype(F32).astype(BF)
    number = within + jnp.dot(rows_before, whole, preferred_element_type=F32)
    spot = jnp.full((LAT, LON), -1.0, F32)
    for m in range(NEXP):
        spot = jnp.where(member == m, number[m * LAT : (m + 1) * LAT] + float(m * CAP), spot)
    place[...] = spot

    row_no = lax.broadcasted_iota(jnp.int32, (LON, 128), 0)

    def lat_step(i, q, south, north, edges, write):
        u = ub[i]
        v = vb[i]
        for a, b in LANES:
            n = b - a
            mid = q[i, :, a:b].astype(F32)
            down = south(a, b)
            up = north(a, b)
            west = pltpu.roll(mid, 1, 0)
            east = pltpu.roll(mid, LON - 1, 0)
            rn = row_no[:, :n]
            west = jnp.where(rn == 0, edges[1, i, 0:1, a:b], west)
            east = jnp.where(rn == LON - 1, edges[0, i, 0:1, a:b], east)
            uu, vv = u[:, :n], v[:, :n]
            lon_up = jnp.where(uu > 0, west, east)
            lat_up = jnp.where(vv > 0, down, up)
            new = mid + jnp.abs(uu) * (lon_up - mid) + jnp.abs(vv) * (lat_up - mid)
            write(i, a, b, new)

    def advance(q, step, write, points):
        def row(i):
            return lambda a, b: q[i, :, a:b].astype(F32)

        def south_halo(a, b):
            return jnp.where(t == 0, 0.0, nsh[2 * step + 1, :, a:b].astype(F32))

        def north_halo(a, b):
            return jnp.where(t == NTILE - 1, 0.0, nsh[2 * step, :, a:b].astype(F32))

        edges = ewfr
        h = halo0 if step == 0 else halo1
        h[2].wait_recv()
        h[3].wait_recv()
        for n in range(2):
            both = ewr[2 * step + n].astype(F32)
            for i in range(LAT):
                ewfr[n, i] = jnp.broadcast_to(both[i : i + 1], (8, F))

        def inner(i, carry):
            lat_step(i, q, row(i - 1), row(i + 1), edges, write)
            points(i)
            return carry

        lax.fori_loop(1, LAT - 1, inner, 0)
        h[0].wait_recv()
        h[1].wait_recv()
        lat_step(0, q, south_halo, row(1), edges, write)
        lat_step(LAT - 1, q, row(LAT - 2), north_halo, edges, write)

    def write_first(i, a, b, new):
        q1[i, :, a:b] = new.astype(BF)
        put_edge(0, i, a, b, new[0:1])
        put_edge(1, i, a, b, new[LON - 1 : LON])

    def write_last(i, a, b, new):
        out = new.astype(BF)
        adv[i, :, a:b] = out
        if a == MAIN:
            xt[i, :, 0 : F - MAIN] = out

    def points_first(i):
        @pl.when(i % 4 == 3)
        def _():
            ring_point(i // 4)

    def points_last(i):
        @pl.when(i % 4 == 3)
        def _():
            ring_point(3 + i // 4)

    advance(q0, 0, write_first, points_first)
    ews[2] = ewfs[0].astype(BF)
    ews[3] = ewfs[1].astype(BF)
    for h in (halo1[2], halo1[3], halo1[0], halo1[1]):
        h.start()

    xt[...] = jnp.zeros_like(xt)

    for i in range(LAT):
        pcol[i] = jnp.transpose(jnp.broadcast_to(place[i : i + 1, :], (LON, LON)))
        tend_ref[i] = jnp.zeros((LON, OUTW), BF)

    advance(q1, 1, write_last, points_last)
    ring_point(6)
    cp_adv.start()

    def forward(k):
        return pltpu.make_async_remote_copy(
            send.at[k], recv.at[k], f_s.at[k], f_r.at[k], device_id=dest_id(k), device_id_type=MESH
        )

    def back(k):
        return pltpu.make_async_remote_copy(
            rs.at[k], rr.at[k], r_s.at[k], r_r.at[k], device_id=source_id(k), device_id_type=MESH
        )

    slot_no = lax.broadcasted_iota(jnp.int32, (CAP, LON), 0)

    def pack(gi, carry):
        for b in range(GB):
            wanted = (slot_no + dest_base(gi * GB + b)).astype(F32)
            for i in range(LAT):
                hit = place[i : i + 1, :] == wanted
                pmat[b * CAP : (b + 1) * CAP, i * LON : (i + 1) * LON] = hit.astype(F32).astype(BF)
        main = jnp.dot(
            pmat[...], adv[:, :, 0:MAIN].reshape(COLS, MAIN), preferred_element_type=F32
        )
        tail = jnp.dot(pmat[...], xt[...].reshape(COLS, 128), preferred_element_type=F32)
        for b in range(GB):
            k = gi * GB + b
            for n in range(4):
                part = main[b * CAP : (b + 1) * CAP, n * 128 : (n + 1) * 128]
                send[k, n * CAP : (n + 1) * CAP, :] = part.astype(BF)
            low = tail[b * CAP : b * CAP + CAP // 2]
            high = tail[b * CAP + CAP // 2 : (b + 1) * CAP]
            send[k, 4 * CAP : ROWS_OUT, :] = (low + pltpu.roll(high, 64, 1)).astype(BF)
            if b == 0:

                @pl.when(gi == 0)
                def _():
                    recv[0] = send[0]

                @pl.when(gi > 0)
                def _():
                    forward(k).start()
            else:
                forward(k).start()
        ring_point(ADV_POINTS + gi)
        return carry

    lax.fori_loop(0, NG, pack, 0)
    ring_points(ADV_POINTS + NG, POINTS)

    @pl.when((rel == 4) | (rel == 5))
    def _():
        def landed(k, carry):
            wcopy(k, 1, w_s1).wait_recv()
            return carry

        lax.fori_loop(0, CHUNKS, landed, 0)

    def weights(base, rows, parts):
        return jnp.concatenate(
            [wts[base + n * rows : base + (n + 1) * rows, :] for n in range(parts)], axis=1
        )

    def net(gi, carry):
        for b in range(GB):
            k = gi * GB + b
            if b == 0:

                @pl.when(gi > 0)
                def _():
                    forward(k).wait_recv()
            else:
                forward(k).wait_recv()
            for n in range(4):
                xin[b * CAP : (b + 1) * CAP, n * 128 : (n + 1) * 128] = recv[
                    k, n * CAP : (n + 1) * CAP, :
                ]
            both = recv[k, 4 * CAP : ROWS_OUT, :]
            xin[b * CAP : b * CAP + CAP // 2, MAIN:640] = both
            xin[b * CAP + CAP // 2 : (b + 1) * CAP, MAIN:640] = pltpu.roll(
                both.astype(F32), 64, 1
            ).astype(BF)
        h = jnp.dot(xin[:, 0:KIN], weights(0, KIN, 4), preferred_element_type=F32)
        h = jnp.maximum(h, 0.15 * h).astype(BF)
        for layer in range(NMID):
            w = weights(W_MID + layer * 4 * HID, HID, 4)
            h = jnp.dot(h, w, preferred_element_type=F32)
            h = jnp.maximum(h, 0.15 * h).astype(BF)
        out = jnp.dot(h, weights(W_OUT, HID, 3), preferred_element_type=F32).astype(BF)
        for b in range(GB):
            k = gi * GB + b
            for n in range(3):
                rs[k, n * CAP : (n + 1) * CAP, :] = out[
                    b * CAP : (b + 1) * CAP, n * 128 : (n + 1) * 128
                ]
            if b == 0:

                @pl.when(gi == 0)
                def _():
                    rr[0] = rs[0]

                @pl.when(gi > 0)
                def _():
                    back(k).start()
            else:
                back(k).start()
        return carry

    lax.fori_loop(0, NG, net, 0)

    lane_no = lax.broadcasted_iota(jnp.int32, (1, GB * CAP), 1)

    def unpack(gi, carry):
        blocks = []
        wanted = lane_no
        for b in range(GB):
            k = gi * GB + b
            if b == 0:

                @pl.when(gi > 0)
                def _():
                    back(k).wait_recv()
            else:
                back(k).wait_recv()
            blocks.append(
                jnp.concatenate([rr[k, n * CAP : (n + 1) * CAP, :] for n in range(3)], axis=1)
            )
            mine = (lane_no >= b * CAP) & (lane_no < (b + 1) * CAP)
            wanted = jnp.where(mine, lane_no - b * CAP + dest_base(k), wanted)
        block = jnp.concatenate(blocks, axis=0)
        wanted = wanted.astype(F32)

        def lats(i, carry):
            hits = []
            for s in range(4):
                col = pcol[i * 4 + s]
                hits.append(
                    jnp.concatenate(
                        [
                            (col == wanted[:, n * 128 : (n + 1) * 128]).astype(F32).astype(BF)
                            for n in range(3)
                        ],
                        axis=1,
                    )
                )
            got = jnp.dot(jnp.concatenate(hits, axis=0), block, preferred_element_type=F32)
            for s in range(4):
                old = tend_ref[i * 4 + s].astype(F32)
                new = old + got[s * LON : (s + 1) * LON, 0:OUTW]
                tend_ref[i * 4 + s] = new.astype(BF)
            return carry

        lax.fori_loop(0, LAT // 4, lats, 0)
        return carry

    lax.fori_loop(0, NG, unpack, 0)

    for h in halo0 + halo1:
        h.wait_send()

    def sent(k, carry):
        forward(k).wait_send()
        back(k).wait_send()
        return carry

    lax.fori_loop(1, NEXP, sent, 0)

    def passed_on(k, carry):
        wcopy(k, 1, w_s1).wait_send()
        return carry

    @pl.when((rel != 4) & (rel != 5))
    def _():
        lax.fori_loop(0, CHUNKS, passed_on, 0)

    @pl.when(rel == 0)
    def _():
        def passed_down(k, carry):
            wcopy(k, -1, w_s2).wait_send()
            return carry

        lax.fori_loop(0, CHUNKS, passed_down, 0)

    cp_adv.wait()


def on_device(state, courant, route, counts, w_in, w_mid, w_out):
    anywhere = pl.BlockSpec(memory_space=pl.ANY)
    vmem = pl.BlockSpec(memory_space=pltpu.VMEM)
    dma = pltpu.SemaphoreType.DMA
    scratch = [
        pltpu.VMEM((LAT, LON, F), BF),
        pltpu.VMEM((LAT, LON, F), BF),
        pltpu.VMEM((LAT, LON, F), BF),
        pltpu.VMEM((LAT, LON, 128), BF),
        pltpu.VMEM((LAT, LON, 2), BF),
        pltpu.VMEM((LAT, LON, 128), F32),
        pltpu.VMEM((LAT, LON, 128), F32),
        pltpu.VMEM((4, LON, F), BF),
        pltpu.VMEM((4, LAT, F), BF),
        pltpu.VMEM((4, LAT, F), BF),
        pltpu.VMEM((2, LAT, F), F32),
        pltpu.VMEM((2, LAT, 8, F), F32),
        pltpu.VMEM((LAT, LON), F32),
        pltpu.VMEM((LAT, LON, 128), F32),
        pltpu.VMEM((GB * CAP, COLS), BF),
        pltpu.VMEM((NEXP, ROWS_OUT, 128), BF),
        pltpu.VMEM((NEXP, ROWS_OUT, 128), BF),
        pltpu.VMEM((NEXP, ROWS_RET, 128), BF),
        pltpu.VMEM((NEXP, ROWS_RET, 128), BF),
        pltpu.VMEM((W_ROWS, 128), BF),
        pltpu.VMEM((1, F, HID), BF),
        pltpu.VMEM((1, NMID, HID, HID), BF),
        pltpu.VMEM((1, HID, OUTW), BF),
        pltpu.VMEM((GB * CAP, 640), BF),
        dma((6,)),
        dma((8,)),
        dma((8,)),
        dma((CHUNKS,)),
        dma((CHUNKS,)),
        dma((CHUNKS,)),
        dma((NEXP,)),
        dma((NEXP,)),
        dma((NEXP,)),
        dma((NEXP,)),
    ]
    return pl.pallas_call(
        kernel,
        out_shape=(
            jax.ShapeDtypeStruct((LAT, LON, F), BF),
            jax.ShapeDtypeStruct((LAT, LON, OUTW), BF),
        ),
        in_specs=[pl.BlockSpec(memory_space=pltpu.SMEM), vmem] + [anywhere] * 5,
        out_specs=(anywhere, vmem),
        scratch_shapes=scratch,
        compiler_params=pltpu.CompilerParams(
            collective_id=0, has_side_effects=True, vmem_limit_bytes=60 * 2**20
        ),
        name="step",
    )(counts, route.reshape(LAT, LON), state, courant, w_in, w_mid, w_out)


def solution(mesh):
    in_specs = (
        P("tile", "grp", None),
        P("tile", "grp", None),
        P("tile", "grp", None, None),
        P("tile"),
        P("tile", None, None),
        P("tile", None, None, None),
        P("tile", None, None),
    )
    out_specs = (P("tile", "grp", None), P("tile", "grp", None))
    return jax.shard_map(
        on_device, mesh=mesh, in_specs=in_specs, out_specs=out_specs, check_vma=False
    )
```

time: 399 us -> 122 us (0.31)
  the two profiles are of different devices: /device:TPU:6 before, /device:TPU:1 now
where the time goes in v1:
time: 122 us; the launch traced here: 120 us
  Pallas kernels  104 us (85%)
  local copies, waits for them, and re-layouts  14.9 us (12%)
    pallas_call x1, Pallas kernels, on_device(): pl.pallas_call(kernel, out_shape=(jax.ShapeDtypeStruct((LAT, LON, F), BF)...  104 us
    unnamed x5, local copies, waits for them, and re-layouts  8.5 us
    pallas_call x2, local copies, waits for them, and re-layouts, on_device(): pl.pallas_call(kernel, out_shape=(jax.ShapeDtypeStruct((LAT, LON, F), BF)...  6.43 us

profile of v1, /device:TPU:1, one launch (start us, length us, event | category | flops | bytes accessed | tf_op | source)
XLA Modules:
  0.0 119.6 jit_solution(12993933178351693541)
XLA Ops:
  0.6 1.9 %copy.11.wout_hbm = bf16[1,512,368]{2,1,0:T(8,128)(2,1)} copy(bf16[1,512,368]{1,2,0:T(8,128)(2,1)} %param.13) | data formatting | bytes 753664 | tf_op args[6]
  2.5 1.8 %copy.10.cour_hbm = bf16[16,128,2]{2,1,0:T(8,128)(2,1)} copy(bf16[16,128,2]{1,2,0:T(2,128)(2,1)} %param.8) | data formatting | bytes 16384 | tf_op args[1]
  4.3 4.8 %copy.9.state_hbm = bf16[16,128,556]{2,1,0:T(8,128)(2,1)} copy(bf16[16,128,556]{1,0,2:T(8,128)(2,1)} %param.7) | data formatting | bytes 4554752 | tf_op args[0]
  9.1 104.0 %step.1 = (bf16[16,128,556]{2,1,0:T(8,128)(2,1)}, bf16[16,128,368]{2,1,0:T(8,128)(2,1)}) custom-call(s32[16]{0:T(128)} %counts_ref.1, s32[16,128]{1,0:T(8,128)} %bitcast.1, bf16[16,128,556]{2,1,0:T(8,128)(2,1)} %copy.9.state_hbm, bf16[16,128,2]{2,1,0:T(8,128)(2,1)} %copy.10.cour_hbm, bf16[1,556,512]{2,1,0:T(8,128)(2,1)} %win_hbm.1, ...), custom_call_target="tpu_custom_call" | custom-call | tf_op jit(solution)/shard_map/step/pallas_call | solution.py:534
  113.1 0.0 copy-start
  113.1 4.8 %copy.12 = bf16[16,128,556]{1,0,2:T(8,128)(2,1)} copy(bf16[16,128,556]{2,1,0:T(8,128)(2,1)} %get-tuple-element.2) | data formatting | bytes 4554752 | tf_op jit(solution)/shard_map/step/pallas_call | solution.py:534
  118.0 0.0 copy-done
  118.0 1.6 %copy.13 = bf16[16,128,368]{1,2,0:T(8,128)(2,1)} copy(bf16[16,128,368]{2,1,0:T(8,128)(2,1)S(1)} %copy-done) | data formatting | bytes 3014656 | tf_op jit(solution)/shard_map/step/pallas_call | solution.py:534
Async XLA Ops:
  113.1 4.8 %copy-start = (bf16[16,128,368]{2,1,0:T(8,128)(2,1)S(1)}, bf16[16,128,368]{2,1,0:T(8,128)(2,1)}, u32[]{:S(2)}) copy-start(bf16[16,128,368]{2,1,0:T(8,128)(2,1)} %get-tuple-element.3) | copy-start | bytes 4521988

commit v2 on v1

v2 whole, which is shorter than its diff:
```python
import jax
import jax.numpy as jnp
from jax import lax
from jax.experimental import pallas as pl
from jax.experimental.pallas import tpu as pltpu
from jax.sharding import PartitionSpec as P

BF = jnp.bfloat16
F32 = jnp.float32
MESH = pl.DeviceIdType.MESH

F, HID, OUTW, NMID = 556, 512, 368, 3
FP = 560
FZ = 640
OUTP = 384
LAT, LON, COLS = 16, 128, 2048
CAP = 96
NEXP = 32
NTILE = 32
MAIN = 512
KIN = 576
PARTS = ((0, 256), (256, FP))
ROWS_A = 2 * CAP
ROWS_B = 2 * CAP + CAP // 2
ROWS_RET = 3 * CAP
W_MID = 4 * KIN
W_OUT = W_MID + NMID * 4 * HID
W_ROWS = W_OUT + 4 * OUTP
CHUNKS = 24
CH = W_ROWS // CHUNKS
LAG = 2
GB = 4
NG = NEXP // GB
SLOTS = GB * CAP
FIRST = 3
EARLY = 4
POINTS = CHUNKS + 3 * LAG


def transposed_dot(a, b):
    return lax.dot_general(a, b, (((1,), (1,)), ((), ())), preferred_element_type=F32)


def kernel(
    counts_hbm, route_hbm, state_hbm, cour_hbm, win_hbm, wmid_hbm, wout_hbm,
    adv_hbm, tend_hbm,
    counts_ref, route_ref, tend_ref,
    st, q32, q0, q1, adv, cour, sel, lon, nsh, xs, xr, hx, place, pall,
    send_a, recv_a, send_b, recv_b, rs, rr, wts, wi, wm, wo, xin, rt,
    lsem, hs_sem, hr_sem, w_s1, w_s2, w_r, fa_s, fa_r, fb_s, fb_r, r_s, r_r,
):
    t = lax.axis_index("tile")
    g = lax.axis_index("grp")
    y, z, x, c = t // 8, t % 8, g // 2, g % 2

    def dest(k):
        j = lax.rem(k * 13, NEXP)
        return lax.rem(y + j // 8, 4), lax.rem(x + (j // 2) % 4, 4), lax.rem(c + j % 2, 2)

    def dest_id(k):
        ty, tx, tc = dest(k)
        return {"tile": ty * 8 + z, "grp": tx * 2 + tc}

    def dest_base(k):
        ty, tx, tc = dest(k)
        return (ty * 8 + tx + 4 * tc) * CAP

    def source_id(k):
        j = lax.rem(k * 13, NEXP)
        ty = lax.rem(y + 4 - j // 8, 4)
        tx = lax.rem(x + 4 - (j // 2) % 4, 4)
        return {"tile": ty * 8 + z, "grp": tx * 2 + lax.rem(c + j % 2, 2)}

    def ring_id(d):
        return {"tile": y * 8 + lax.rem(z + d + 8, 8)}

    def tile_id(d):
        return {"tile": lax.rem(t + d + NTILE, NTILE)}

    def grp_id(d):
        return {"grp": lax.rem(g + d + 8, 8)}

    rel = lax.rem(z + 8 - (x + 4 * c), 8)
    forward_up = (rel >= 1) & (rel <= 3)
    forward_down = rel >= 6
    hop = jnp.where(rel <= 4, rel, 8 - rel)

    barrier = pltpu.get_barrier_semaphore()

    def greet(k, carry):
        pl.semaphore_signal(barrier, inc=1, device_id=dest_id(k), device_id_type=MESH)
        return carry

    lax.fori_loop(1, NEXP, greet, 0)
    for d in (1, -1):
        pl.semaphore_signal(barrier, inc=1, device_id=ring_id(d), device_id_type=MESH)
        pl.semaphore_signal(barrier, inc=1, device_id=tile_id(d), device_id_type=MESH)
        pl.semaphore_signal(barrier, inc=1, device_id=grp_id(d), device_id_type=MESH)

    cp_state = pltpu.make_async_copy(state_hbm, st, lsem.at[0])
    cp_cour = pltpu.make_async_copy(cour_hbm, cour, lsem.at[1])
    cp_wi = pltpu.make_async_copy(win_hbm, wi, lsem.at[2])
    cp_wm = pltpu.make_async_copy(wmid_hbm, wm, lsem.at[3])
    cp_wo = pltpu.make_async_copy(wout_hbm, wo, lsem.at[4])
    cp_adv = pltpu.make_async_copy(st, adv_hbm, lsem.at[5])
    cp_tend = pltpu.make_async_copy(tend_ref, tend_hbm, lsem.at[6])
    cp_counts = pltpu.make_async_copy(counts_hbm, counts_ref, lsem.at[7])
    cp_route = pltpu.make_async_copy(route_hbm, route_ref, lsem.at[8])
    cp_state.start()
    cp_cour.start()
    cp_counts.start()
    cp_route.start()

    @pl.when(rel == 0)
    def _():
        cp_wi.start()
        cp_wm.start()
        cp_wo.start()

    def halo(n, src, dst, device):
        return pltpu.make_async_remote_copy(
            src, dst, hs_sem.at[n], hr_sem.at[n], device_id=device, device_id_type=MESH
        )

    def halos(step, part, q):
        lo, hi = PARTS[part]
        own = pl.ds(lo, hi - lo)
        b = 8 * step + 4 * part
        return [
            halo(b, q.at[0, own], nsh.at[2 * step, own], tile_id(-1)),
            halo(b + 1, q.at[LAT - 1, own], nsh.at[2 * step + 1, own], tile_id(1)),
            halo(b + 2, xs.at[step, own], xr.at[2 * step + 1, own], grp_id(-1)),
            halo(b + 3, xs.at[step, own], xr.at[2 * step, own], grp_id(1)),
        ]

    halo0 = [halos(0, 0, q0), halos(0, 1, q0)]
    halo1 = [halos(1, 0, q1), halos(1, 1, q1)]

    def wcopy(k, d, sem):
        part = wts.at[pl.ds(pl.multiple_of(k * CH, CH), CH)]
        return pltpu.make_async_remote_copy(
            part, part, sem.at[k], w_r.at[k], device_id=ring_id(d), device_id_type=MESH
        )

    def ring_point(p):
        k = p - LAG * hop
        ok = (k >= 0) & (k < CHUNKS)

        @pl.when(ok & (rel == 0))
        def _():
            wcopy(k, 1, w_s1).start()
            wcopy(k, -1, w_s2).start()

        @pl.when(ok & forward_up)
        def _():
            wcopy(k, 1, w_s1).wait_recv()
            wcopy(k, 1, w_s1).start()

        @pl.when(ok & forward_down)
        def _():
            wcopy(k, -1, w_s1).wait_recv()
            wcopy(k, -1, w_s1).start()

    def ring_points(a, b):
        def one(p, carry):
            ring_point(p)
            return carry

        lax.fori_loop(a, b, one, 0)

    cp_state.wait()

    def widen(i, carry):
        for s in range(4):
            q32[pl.ds(pl.multiple_of((i * 4 + s) * LAT, LAT), LAT), :] = st[i * 4 + s].astype(F32)
        return carry

    lax.fori_loop(0, F // 4, widen, 0)
    q32[F * LAT : FP * LAT, :] = jnp.zeros(((FP - F) * LAT, LON), F32)

    for i in range(LAT):
        q0[i] = q32[pl.ds(i, FP, stride=LAT), :].astype(BF)

    s_row = lax.broadcasted_iota(jnp.int32, (LON, 128), 0)
    s_lane = lax.broadcasted_iota(jnp.int32, (LON, 128), 1)
    for i in range(LAT):
        pick = ((s_row == LON - 1) & (s_lane == i)) | ((s_row == 0) & (s_lane == 64 + i))
        sel[i * LON : (i + 1) * LON, :] = pick.astype(F32).astype(BF)

    def edges(step, part, q):
        lo, hi = PARTS[part]
        row = jnp.concatenate([q[i, lo:hi, :] for i in range(LAT)], axis=1)
        xs[step, lo:hi, :] = jnp.dot(row, sel[...], preferred_element_type=F32).astype(BF)

    edges(0, 0, q0)
    edges(0, 1, q0)

    cp_cour.wait()

    def lon_matrix(i, carry):
        u = cour[i].astype(F32)[0:1]
        pos, neg = jnp.maximum(u, 0.0), jnp.maximum(-u, 0.0)
        top = jnp.where(s_row == s_lane - 1, pos, 0.0)
        top = jnp.where(s_row == s_lane + 1, neg, top)
        top = jnp.where(s_row == s_lane, -(pos + neg), top)
        low = jnp.where((s_row == i) & (s_lane == 0), pos, 0.0)
        low = jnp.where((s_row == 64 + i) & (s_lane == LON - 1), neg, low)
        lon[i, 0:LON, :] = top.astype(BF)
        lon[i, LON : 2 * LON, :] = low.astype(BF)
        return carry

    lax.fori_loop(0, LAT, lon_matrix, 0)

    cp_counts.wait()
    cp_route.wait()

    lat_no = lax.broadcasted_iota(jnp.int32, (LAT, LON), 0)
    lon_no = lax.broadcasted_iota(jnp.int32, (LAT, LON), 1) + g * LON
    reach = jnp.zeros((LAT, LON), jnp.int32)
    for i in range(LAT):
        reach = jnp.where(lat_no == i, counts_ref[i], reach)
    member = jnp.where(lon_no < reach, route_ref[...], -1)
    named = jnp.concatenate([(member == m).astype(F32) for m in range(NEXP)], axis=0).astype(BF)
    before = (
        lax.broadcasted_iota(jnp.int32, (LON, LON), 0)
        < lax.broadcasted_iota(jnp.int32, (LON, LON), 1)
    )
    within = jnp.dot(named, before.astype(F32).astype(BF), preferred_element_type=F32)
    whole = jnp.dot(named, jnp.ones((LON, LON), BF), preferred_element_type=F32).astype(BF)
    r0 = lax.broadcasted_iota(jnp.int32, (NEXP * LAT, NEXP * LAT), 0)
    r1 = lax.broadcasted_iota(jnp.int32, (NEXP * LAT, NEXP * LAT), 1)
    rows_before = ((r0 // LAT == r1 // LAT) & (r1 < r0)).astype(F32).astype(BF)
    number = within + jnp.dot(rows_before, whole, preferred_element_type=F32)
    spot = jnp.full((LAT, LON), -1.0, F32)
    for m in range(NEXP):
        spot = jnp.where(member == m, number[m * LAT : (m + 1) * LAT] + float(m * CAP), spot)
    place[...] = spot

    slot_no = lax.broadcasted_iota(jnp.int32, (CAP, LON), 0)

    def hits(gi, carry):
        for b in range(GB):
            wanted = (slot_no + dest_base(gi * GB + b)).astype(F32)
            for i in range(LAT):
                hit = place[i : i + 1, :] == wanted
                pall[gi, b * CAP : (b + 1) * CAP, i * LON : (i + 1) * LON] = hit.astype(F32).astype(BF)
        return carry

    def lat_step(i, lo, hi, q, south, north, write):
        row = jnp.concatenate([q[i, lo:hi, :], hx[lo:hi, :]], axis=1)
        part = jnp.dot(row, lon[i], preferred_element_type=F32)
        v = cour[i].astype(F32)[1:2]
        half = (hi - lo) // 32 * 16
        for a, b in ((lo, lo + half), (lo + half, hi)):
            mid = q[i, a:b, :].astype(F32)
            lat_up = jnp.where(jnp.broadcast_to(v > 0, (b - a, LON)), south(a, b), north(a, b))
            write(i, a, b, mid + part[a - lo : b - lo] + jnp.abs(v) * (lat_up - mid))

    def advance(q, step, p, write):
        lo, hi = PARTS[p]

        def row(i):
            return lambda a, b: q[i, a:b, :].astype(F32)

        def south_halo(a, b):
            return jnp.where(t == 0, 0.0, nsh[2 * step + 1, a:b, :].astype(F32))

        def north_halo(a, b):
            return jnp.where(t == NTILE - 1, 0.0, nsh[2 * step, a:b, :].astype(F32))

        h = (halo0 if step == 0 else halo1)[p]
        h[2].wait_recv()
        h[3].wait_recv()
        west, east = xr[2 * step, lo:hi].astype(F32), xr[2 * step + 1, lo:hi].astype(F32)
        lane_no = lax.broadcasted_iota(jnp.int32, (hi - lo, 128), 1)
        hx[lo:hi, :] = jnp.where(lane_no < 64, west, east).astype(BF)

        def inner(i, carry):
            lat_step(i, lo, hi, q, row(i - 1), row(i + 1), write)
            return carry

        lax.fori_loop(1, LAT - 1, inner, 0)
        h[0].wait_recv()
        h[1].wait_recv()
        lat_step(0, lo, hi, q, south_halo, row(1), write)
        lat_step(LAT - 1, lo, hi, q, row(LAT - 2), north_halo, write)

    def write_first(i, a, b, new):
        q1[i, a:b, :] = new.astype(BF)

    def write_last(i, a, b, new):
        out = new.astype(BF)
        adv[i, a:b, :] = out
        q32[pl.ds(a * LAT + i, b - a, stride=LAT), :] = out.astype(F32)

    pl.semaphore_wait(barrier, NEXP - 1 + 6)
    for p in range(2):
        for n in (2, 3, 0, 1):
            halo0[p][n].start()

    @pl.when(rel == 0)
    def _():
        cp_wi.wait()
        cp_wm.wait()
        cp_wo.wait()
        for n in range(4):
            wts[n * KIN + 544 : (n + 1) * KIN, :] = jnp.zeros((KIN - 544, 128), BF)
            wts[n * KIN : n * KIN + F, :] = wi[0, :, n * 128 : (n + 1) * 128]
        for k in range(NMID):
            for n in range(4):
                r = W_MID + (k * 4 + n) * HID
                wts[r : r + HID, :] = wm[0, k, :, n * 128 : (n + 1) * 128]
        for n in range(4):
            r = W_OUT + n * OUTP
            wts[r : r + OUTW, :] = wo[0, :, n * 128 : (n + 1) * 128]
            wts[r + OUTW : r + OUTP, :] = jnp.zeros((OUTP - OUTW, 128), BF)

    lax.fori_loop(0, NG, hits, 0)
    for i in range(LAT):
        adv[i, FP:FZ, :] = jnp.zeros((FZ - FP, LON), BF)
        tend_ref[i] = jnp.zeros((OUTW, LON), BF)
    for p in range(2):
        advance(q0, 0, p, write_first)
        halo1[p][0].start()
        halo1[p][1].start()
        edges(1, p, q1)
        halo1[p][2].start()
        halo1[p][3].start()
        ring_point(p)

    def forward(p, k):
        src, dst, s_sem, r_sem = ((send_a, recv_a, fa_s, fa_r), (send_b, recv_b, fb_s, fb_r))[p]
        return pltpu.make_async_remote_copy(
            src.at[k], dst.at[k], s_sem.at[k], r_sem.at[k], device_id=dest_id(k), device_id_type=MESH
        )

    def back(k):
        return pltpu.make_async_remote_copy(
            rs.at[k], rr.at[k], r_s.at[k], r_r.at[k], device_id=source_id(k), device_id_type=MESH
        )

    def launch(p, gi, b):
        k = gi * GB + b
        if b > 0:
            forward(p, k).start()
            return

        @pl.when(gi == 0)
        def _():
            if p == 0:
                recv_a[0] = send_a[0]
            else:
                recv_b[0] = send_b[0]

        @pl.when(gi > 0)
        def _():
            forward(p, k).start()

    def pack_a(gi, carry):
        columns = jnp.concatenate([adv[i, 0:256, :] for i in range(LAT)], axis=1)
        rows = transposed_dot(pall[gi], columns)
        for b in range(GB):
            for n in range(2):
                part = rows[b * CAP : (b + 1) * CAP, n * 128 : (n + 1) * 128]
                send_a[gi * GB + b, n * CAP : (n + 1) * CAP, :] = part.astype(BF)
            launch(0, gi, b)
        ring_point(jnp.where(gi < FIRST, EARLY - 1, EARLY) + gi)
        return carry

    def pack_b(gi, carry):
        columns = jnp.concatenate([adv[i, 256:FZ, :] for i in range(LAT)], axis=1)
        rows = transposed_dot(pall[gi], columns)
        for b in range(GB):
            for n in range(2):
                part = rows[b * CAP : (b + 1) * CAP, n * 128 : (n + 1) * 128]
                send_b[gi * GB + b, n * CAP : (n + 1) * CAP, :] = part.astype(BF)
            low = rows[b * CAP : b * CAP + CAP // 2, 256:384]
            high = rows[b * CAP + CAP // 2 : (b + 1) * CAP, 256:384]
            send_b[gi * GB + b, 2 * CAP : ROWS_B, :] = (low + pltpu.roll(high, 64, 1)).astype(BF)
            launch(1, gi, b)
        ring_point(EARLY + NG + gi)
        return carry

    advance(q1, 1, 0, write_last)
    ring_point(2)
    lax.fori_loop(0, FIRST, pack_a, 0)
    advance(q1, 1, 1, write_last)
    ring_point(EARLY - 1 + FIRST)
    lax.fori_loop(FIRST, NG, pack_a, 0)
    lax.fori_loop(0, NG, pack_b, 0)

    def narrow(i, carry):
        for s in range(4):
            st[i * 4 + s] = q32[pl.ds(pl.multiple_of((i * 4 + s) * LAT, LAT), LAT), :].astype(BF)
        return carry

    lax.fori_loop(0, F // 4, narrow, 0)
    cp_adv.start()
    ring_points(EARLY + 2 * NG, POINTS)

    @pl.when((rel == 4) | (rel == 5))
    def _():
        def landed(k, carry):
            wcopy(k, 1, w_s1).wait_recv()
            return carry

        lax.fori_loop(0, CHUNKS, landed, 0)

    def weights(base, rows, parts):
        return jnp.concatenate(
            [wts[base + n * rows : base + (n + 1) * rows, :] for n in range(parts)], axis=1
        )

    def net(gi, carry):
        for b in range(GB):
            k = gi * GB + b
            if b == 0:

                @pl.when(gi > 0)
                def _():
                    forward(0, k).wait_recv()
                    forward(1, k).wait_recv()
            else:
                forward(0, k).wait_recv()
                forward(1, k).wait_recv()
            own = slice(b * CAP, (b + 1) * CAP)
            for n in range(2):
                xin[own, n * 128 : (n + 1) * 128] = recv_a[k, n * CAP : (n + 1) * CAP, :]
                xin[own, 256 + n * 128 : 384 + n * 128] = recv_b[k, n * CAP : (n + 1) * CAP, :]
            both = recv_b[k, 2 * CAP : ROWS_B, :]
            xin[b * CAP : b * CAP + CAP // 2, MAIN:640] = both
            xin[b * CAP + CAP // 2 : (b + 1) * CAP, MAIN:640] = pltpu.roll(
                both.astype(F32), 64, 1
            ).astype(BF)
        h = jnp.dot(xin[:, 0:KIN], weights(0, KIN, 4), preferred_element_type=F32)
        h = jnp.maximum(h, 0.15 * h).astype(BF)
        for layer in range(NMID):
            w = weights(W_MID + layer * 4 * HID, HID, 4)
            h = jnp.dot(h, w, preferred_element_type=F32)
            h = jnp.maximum(h, 0.15 * h).astype(BF)
        out = transposed_dot(h, weights(W_OUT, OUTP, 4)).astype(BF)
        for b in range(GB):
            k = gi * GB + b
            for n in range(3):
                rs[k, n * CAP : (n + 1) * CAP, :] = out[
                    b * CAP : (b + 1) * CAP, n * 128 : (n + 1) * 128
                ]
            if b == 0:

                @pl.when(gi == 0)
                def _():
                    rr[0] = rs[0]

                @pl.when(gi > 0)
                def _():
                    back(k).start()
            else:
                back(k).start()
        return carry

    lax.fori_loop(0, NG, net, 0)

    def unpack(gi, carry):
        for b in range(GB):
            k = gi * GB + b
            if b == 0:

                @pl.when(gi > 0)
                def _():
                    back(k).wait_recv()
            else:
                back(k).wait_recv()
        block = jnp.concatenate(
            [
                jnp.concatenate(
                    [rr[gi * GB + b, n * CAP : (n + 1) * CAP, :] for n in range(3)], axis=1
                )
                for b in range(GB)
            ],
            axis=0,
        )
        rt[...] = jnp.transpose(block.astype(F32)).astype(BF)[0:OUTW]
        for i in range(0, LAT, 4):
            got = jnp.dot(
                rt[...], pall[gi, :, i * LON : (i + 4) * LON], preferred_element_type=F32
            )
            for s in range(4):
                old = tend_ref[i + s].astype(F32)
                tend_ref[i + s] = (old + got[:, s * LON : (s + 1) * LON]).astype(BF)
        return carry

    lax.fori_loop(0, NG, unpack, 0)

    cp_tend.start()
    for hs in halo0 + halo1:
        for h in hs:
            h.wait_send()

    def sent(k, carry):
        forward(0, k).wait_send()
        forward(1, k).wait_send()
        back(k).wait_send()
        return carry

    lax.fori_loop(1, NEXP, sent, 0)

    def passed_on(k, carry):
        wcopy(k, 1, w_s1).wait_send()
        return carry

    @pl.when((rel != 4) & (rel != 5))
    def _():
        lax.fori_loop(0, CHUNKS, passed_on, 0)

    @pl.when(rel == 0)
    def _():
        def passed_down(k, carry):
            wcopy(k, -1, w_s2).wait_send()
            return carry

        lax.fori_loop(0, CHUNKS, passed_down, 0)

    cp_adv.wait()
    cp_tend.wait()


def copy_kernel(adv_in, tend_in, adv_out, tend_out, adv_v, tend_v, sem_in, sem_out):
    into, out = [], []
    for j, (a, v, b, n) in enumerate(
        ((adv_in, adv_v, adv_out, F // 4), (tend_in, tend_v, tend_out, LAT // 4))
    ):
        for i in range(4):
            part = pl.ds(i * n, n)
            into.append(pltpu.make_async_copy(a.at[part], v.at[part], sem_in.at[4 * j + i]))
            out.append(pltpu.make_async_copy(v.at[part], b.at[part], sem_out.at[4 * j + i]))
    for one in into:
        one.start()
    for one, two in zip(into, out):
        one.wait()
        two.start()
    for two in out:
        two.wait()


def on_device(state, courant, route, counts, w_in, w_mid, w_out):
    anywhere = pl.BlockSpec(memory_space=pl.ANY)
    dma = pltpu.SemaphoreType.DMA
    scratch = [
        pltpu.SMEM((LAT,), jnp.int32),
        pltpu.VMEM((LAT, LON), jnp.int32),
        pltpu.VMEM((LAT, OUTW, LON), BF),
        pltpu.VMEM((F, LAT, LON), BF),
        pltpu.VMEM((FP * LAT, LON), F32),
        pltpu.VMEM((LAT, FP, LON), BF),
        pltpu.VMEM((LAT, FP, LON), BF),
        pltpu.VMEM((LAT, FZ, LON), BF),
        pltpu.VMEM((LAT, 2, LON), BF),
        pltpu.VMEM((COLS, 128), BF),
        pltpu.VMEM((LAT, 2 * LON, LON), BF),
        pltpu.VMEM((4, FP, LON), BF),
        pltpu.VMEM((2, FP, 128), BF),
        pltpu.VMEM((4, FP, 128), BF),
        pltpu.VMEM((FP, 128), BF),
        pltpu.VMEM((LAT, LON), F32),
        pltpu.VMEM((NG, SLOTS, COLS), BF),
        pltpu.VMEM((NEXP, ROWS_A, 128), BF),
        pltpu.VMEM((NEXP, ROWS_A, 128), BF),
        pltpu.VMEM((NEXP, ROWS_B, 128), BF),
        pltpu.VMEM((NEXP, ROWS_B, 128), BF),
        pltpu.VMEM((NEXP, ROWS_RET, 128), BF),
        pltpu.VMEM((NEXP, ROWS_RET, 128), BF),
        pltpu.VMEM((W_ROWS, 128), BF),
        pltpu.VMEM((1, F, HID), BF),
        pltpu.VMEM((1, NMID, HID, HID), BF),
        pltpu.VMEM((1, OUTW, HID), BF),
        pltpu.VMEM((SLOTS, FZ), BF),
        pltpu.VMEM((OUTW, SLOTS), BF),
        dma((9,)),
        dma((16,)),
        dma((16,)),
        dma((CHUNKS,)),
        dma((CHUNKS,)),
        dma((CHUNKS,)),
        dma((NEXP,)),
        dma((NEXP,)),
        dma((NEXP,)),
        dma((NEXP,)),
        dma((NEXP,)),
        dma((NEXP,)),
    ]
    adv, tend = pl.pallas_call(
        kernel,
        out_shape=(
            jax.ShapeDtypeStruct((F, LAT, LON), BF),
            jax.ShapeDtypeStruct((LAT, OUTW, LON), BF),
        ),
        in_specs=[anywhere] * 7,
        out_specs=(anywhere, anywhere),
        scratch_shapes=scratch,
        compiler_params=pltpu.CompilerParams(
            collective_id=0, has_side_effects=True, vmem_limit_bytes=60 * 2**20
        ),
        name="step",
    )(
        counts,
        route.reshape(LAT, LON),
        jnp.transpose(state, (2, 0, 1)),
        jnp.transpose(courant, (0, 2, 1)),
        w_in,
        w_mid,
        jnp.transpose(w_out, (0, 2, 1)),
    )
    adv, tend = pl.pallas_call(
        copy_kernel,
        out_shape=(
            jax.ShapeDtypeStruct(adv.shape, BF),
            jax.ShapeDtypeStruct(tend.shape, BF),
        ),
        in_specs=[anywhere] * 2,
        out_specs=(anywhere, anywhere),
        scratch_shapes=[
            pltpu.VMEM(adv.shape, BF),
            pltpu.VMEM(tend.shape, BF),
            dma((8,)),
            dma((8,)),
        ],
        name="hand_over",
    )(adv, tend)
    return jnp.transpose(adv, (1, 2, 0)), jnp.transpose(tend, (0, 2, 1))


def solution(mesh):
    in_specs = (
        P("tile", "grp", None),
        P("tile", "grp", None),
        P("tile", "grp", None, None),
        P("tile"),
        P("tile", None, None),
        P("tile", None, None, None),
        P("tile", None, None),
    )
    out_specs = (P("tile", "grp", None), P("tile", "grp", None))
    return jax.shard_map(
        on_device, mesh=mesh, in_specs=in_specs, out_specs=out_specs, check_vma=False
    )
```

time: 122 us -> 110 us (0.902)
  the two profiles are of different devices: /device:TPU:1 before, /device:TPU:37 now
where the time goes in v2:
time: 110 us
  Pallas kernels  109 us (99%)
    pallas_call x1, Pallas kernels, on_device(): pl.pallas_call(kernel, out_shape=(jax.ShapeDtypeStruct((F, LAT, LON), BF)...  106 us
    pallas_call x1, Pallas kernels, on_device(): pl.pallas_call(copy_kernel, out_shape=(jax.ShapeDtypeStruct(adv.shape, BF...  3.06 us

profile of v2, /device:TPU:37, one launch (start us, length us, event | category | flops | bytes accessed | tf_op | source)
XLA Modules:
  0.0 110.0 jit_solution(14571612441929109275)
XLA Ops:
  0.6 106.3 %step.1 = (bf16[556,16,128]{2,1,0:T(8,128)(2,1)}, bf16[16,368,128]{2,1,0:T(8,128)(2,1)}) custom-call(s32[16]{0:T(128)} %counts_hbm.1, s32[16,128]{1,0:T(8,128)} %bitcast.8, bf16[556,16,128]{2,1,0:T(8,128)(2,1)} %bitcast.6, bf16[16,2,128]{2,1,0:T(2,128)(2,1)} %bitcast.9, bf16[1,556,512]{2,1,0:T(8,128)(2,1)} %win_hbm.1, bf16[1,3,512,512]{3,2,1,0:T(8,128)(2,1)} %wmid_hbm.1, ...), custom_call_target="tpu_custom_call" | custom-call | tf_op jit(solution)/shard_map/step/pallas_call | solution.py:591
  107.0 3.1 %hand_over.1 = (bf16[556,16,128]{2,1,0:T(8,128)(2,1)}, bf16[16,368,128]{2,1,0:T(8,128)(2,1)}) custom-call(bf16[556,16,128]{2,1,0:T(8,128)(2,1)} %get-tuple-element.6.adv_in, bf16[16,368,128]{2,1,0:T(8,128)(2,1)} %get-tuple-element.7.tend_in), custom_call_target="tpu_custom_call" | custom-call | tf_op jit(solution)/shard_map/hand_over/pallas_call | solution.py:613

commit v3 on v2

--- a/solution.py
+++ b/solution.py
@@ -28,13 +28,12 @@
 W_ROWS = W_OUT + 4 * OUTP
 CHUNKS = 24
 CH = W_ROWS // CHUNKS
-LAG = 2
+AHEAD = 3
+T_CHUNK, T_HOP, T_RELAY = 12, 52, 175
 GB = 4
 NG = NEXP // GB
 SLOTS = GB * CAP
 FIRST = 3
-EARLY = 4
-POINTS = CHUNKS + 3 * LAG
 
 
 def transposed_dot(a, b):
@@ -142,31 +141,35 @@
             part, part, sem.at[k], w_r.at[k], device_id=ring_id(d), device_id_type=MESH
         )
 
-    def ring_point(p):
-        k = p - LAG * hop
-        ok = (k >= 0) & (k < CHUNKS)
-
-        @pl.when(ok & (rel == 0))
+    def pass_on(k, carry):
+        @pl.when(rel == 0)
         def _():
             wcopy(k, 1, w_s1).start()
             wcopy(k, -1, w_s2).start()
 
-        @pl.when(ok & forward_up)
+        @pl.when(forward_up)
         def _():
             wcopy(k, 1, w_s1).wait_recv()
             wcopy(k, 1, w_s1).start()
 
-        @pl.when(ok & forward_down)
+        @pl.when(forward_down)
         def _():
             wcopy(k, -1, w_s1).wait_recv()
             wcopy(k, -1, w_s1).start()
 
-    def ring_points(a, b):
-        def one(p, carry):
-            ring_point(p)
-            return carry
-
-        lax.fori_loop(a, b, one, 0)
+        return carry
+
+    def passed_by(clock):
+        behind = clock - T_RELAY - T_HOP * (hop - 1)
+        relayed = jnp.where(behind < 0, 0, jnp.minimum(AHEAD + behind // T_CHUNK, CHUNKS))
+        begun = jnp.where(clock >= 40, AHEAD, 0)
+        begun = jnp.where(clock >= 90, 11, begun)
+        begun = jnp.where(clock >= 170, 18, begun)
+        begun = jnp.where(clock >= 210, CHUNKS, begun)
+        return jnp.where(rel == 0, begun, jnp.where(forward_up | forward_down, relayed, 0))
+
+    def ring(before, now):
+        lax.fori_loop(passed_by(before), passed_by(now), pass_on, 0)
 
     cp_state.wait()
 
@@ -319,6 +322,7 @@
     for i in range(LAT):
         adv[i, FP:FZ, :] = jnp.zeros((FZ - FP, LON), BF)
         tend_ref[i] = jnp.zeros((OUTW, LON), BF)
+    ring(0, 40)
     for p in range(2):
         advance(q0, 0, p, write_first)
         halo1[p][0].start()
@@ -326,7 +330,7 @@
         edges(1, p, q1)
         halo1[p][2].start()
         halo1[p][3].start()
-        ring_point(p)
+        ring((40, 65)[p], (65, 90)[p])
 
     def forward(p, k):
         src, dst, s_sem, r_sem = ((send_a, recv_a, fa_s, fa_r), (send_b, recv_b, fb_s, fb_r))[p]
@@ -364,7 +368,8 @@
                 part = rows[b * CAP : (b + 1) * CAP, n * 128 : (n + 1) * 128]
                 send_a[gi * GB + b, n * CAP : (n + 1) * CAP, :] = part.astype(BF)
             launch(0, gi, b)
-        ring_point(jnp.where(gi < FIRST, EARLY - 1, EARLY) + gi)
+        start = jnp.where(gi < FIRST, 170, 180) + 8 * gi
+        ring(start, start + 8)
         return carry
 
     def pack_b(gi, carry):
@@ -378,14 +383,14 @@
             high = rows[b * CAP + CAP // 2 : (b + 1) * CAP, 256:384]
             send_b[gi * GB + b, 2 * CAP : ROWS_B, :] = (low + pltpu.roll(high, 64, 1)).astype(BF)
             launch(1, gi, b)
-        ring_point(EARLY + NG + gi)
+        ring(244 + 10 * gi, 254 + 10 * gi)
         return carry
 
     advance(q1, 1, 0, write_last)
-    ring_point(2)
+    ring(90, 170)
     lax.fori_loop(0, FIRST, pack_a, 0)
     advance(q1, 1, 1, write_last)
-    ring_point(EARLY - 1 + FIRST)
+    ring(170 + 8 * FIRST, 180 + 8 * FIRST)
     lax.fori_loop(FIRST, NG, pack_a, 0)
     lax.fori_loop(0, NG, pack_b, 0)
 
@@ -396,7 +401,7 @@
 
     lax.fori_loop(0, F // 4, narrow, 0)
     cp_adv.start()
-    ring_points(EARLY + 2 * NG, POINTS)
+    ring(244 + 10 * NG, 2000)
 
     @pl.when((rel == 4) | (rel == 5))
     def _():

time: 110 us -> 107 us (0.973)
  the two profiles are of different devices: /device:TPU:37 before, /device:TPU:1 now
where the time goes in v3:
time: 107 us; the launch traced here: 106 us
  Pallas kernels  105 us (98%)
    pallas_call x1, Pallas kernels, on_device(): pl.pallas_call(kernel, out_shape=(jax.ShapeDtypeStruct((F, LAT, LON), BF)...  102 us
    pallas_call x1, Pallas kernels, on_device(): pl.pallas_call(copy_kernel, out_shape=(jax.ShapeDtypeStruct(adv.shape, BF...  3.06 us

profile of v3, /device:TPU:1, one launch (start us, length us, event | category | flops | bytes accessed | tf_op | source)
XLA Modules:
  0.0 105.6 jit_solution(13445895516548982181)
XLA Ops:
  0.6 101.9 %step.1 = (bf16[556,16,128]{2,1,0:T(8,128)(2,1)}, bf16[16,368,128]{2,1,0:T(8,128)(2,1)}) custom-call(s32[16]{0:T(128)} %counts_hbm.1, s32[16,128]{1,0:T(8,128)} %bitcast.8, bf16[556,16,128]{2,1,0:T(8,128)(2,1)} %bitcast.6, bf16[16,2,128]{2,1,0:T(2,128)(2,1)} %bitcast.9, bf16[1,556,512]{2,1,0:T(8,128)(2,1)} %win_hbm.1, bf16[1,3,512,512]{3,2,1,0:T(8,128)(2,1)} %wmid_hbm.1, ...), custom_call_target="tpu_custom_call" | custom-call | tf_op jit(solution)/shard_map/step/pallas_call | solution.py:596
  102.5 3.1 %hand_over.1 = (bf16[556,16,128]{2,1,0:T(8,128)(2,1)}, bf16[16,368,128]{2,1,0:T(8,128)(2,1)}) custom-call(bf16[556,16,128]{2,1,0:T(8,128)(2,1)} %get-tuple-element.6.adv_in, bf16[16,368,128]{2,1,0:T(8,128)(2,1)} %get-tuple-element.7.tend_in), custom_call_target="tpu_custom_call" | custom-call | tf_op jit(solution)/shard_map/hand_over/pallas_call | solution.py:618

commit v4 on v3

--- a/solution.py
+++ b/solution.py
@@ -53,7 +53,7 @@
     y, z, x, c = t // 8, t % 8, g // 2, g % 2
 
     def dest(k):
-        j = lax.rem(k * 13, NEXP)
+        j = lax.rem(k * 5, NEXP)
         return lax.rem(y + j // 8, 4), lax.rem(x + (j // 2) % 4, 4), lax.rem(c + j % 2, 2)
 
     def dest_id(k):
@@ -65,7 +65,7 @@
         return (ty * 8 + tx + 4 * tc) * CAP
 
     def source_id(k):
-        j = lax.rem(k * 13, NEXP)
+        j = lax.rem(k * 5, NEXP)
         ty = lax.rem(y + 4 - j // 8, 4)
         tx = lax.rem(x + 4 - (j // 2) % 4, 4)
         return {"tile": ty * 8 + z, "grp": tx * 2 + lax.rem(c + j % 2, 2)}
@@ -102,7 +102,11 @@
     cp_wm = pltpu.make_async_copy(wmid_hbm, wm, lsem.at[3])
     cp_wo = pltpu.make_async_copy(wout_hbm, wo, lsem.at[4])
     cp_adv = pltpu.make_async_copy(st, adv_hbm, lsem.at[5])
-    cp_tend = pltpu.make_async_copy(tend_ref, tend_hbm, lsem.at[6])
+    cp_tend = []
+    for i in range(0, LAT, 4):
+        own = pl.ds(i, 4)
+        sem = lsem.at[9 + i // 4]
+        cp_tend.append(pltpu.make_async_copy(tend_ref.at[own], tend_hbm.at[own], sem))
     cp_counts = pltpu.make_async_copy(counts_hbm, counts_ref, lsem.at[7])
     cp_route = pltpu.make_async_copy(route_hbm, route_ref, lsem.at[8])
     cp_state.start()
@@ -465,6 +469,35 @@
 
     lax.fori_loop(0, NG, net, 0)
 
+    for hs in halo0 + halo1:
+        for h in hs:
+            h.wait_send()
+
+    def sent(k, carry):
+        forward(0, k).wait_send()
+        forward(1, k).wait_send()
+        return carry
+
+    lax.fori_loop(1, NEXP, sent, 0)
+
+    def passed_on(k, carry):
+        wcopy(k, 1, w_s1).wait_send()
+        return carry
+
+    @pl.when((rel != 4) & (rel != 5))
+    def _():
+        lax.fori_loop(0, CHUNKS, passed_on, 0)
+
+    @pl.when(rel == 0)
+    def _():
+        def passed_down(k, carry):
+            wcopy(k, -1, w_s2).wait_send()
+            return carry
+
+        lax.fori_loop(0, CHUNKS, passed_down, 0)
+
+    cp_adv.wait()
+
     def unpack(gi, carry):
         for b in range(GB):
             k = gi * GB + b
@@ -492,41 +525,26 @@
             for s in range(4):
                 old = tend_ref[i + s].astype(F32)
                 tend_ref[i + s] = (old + got[:, s * LON : (s + 1) * LON]).astype(BF)
+
+            @pl.when(gi == NG - 1)
+            def _():
+                cp_tend[i // 4].start()
+
+        for b in range(GB):
+            k = gi * GB + b
+            if b == 0:
+
+                @pl.when(gi > 0)
+                def _():
+                    back(k).wait_send()
+            else:
+                back(k).wait_send()
         return carry
 
     lax.fori_loop(0, NG, unpack, 0)
 
-    cp_tend.start()
-    for hs in halo0 + halo1:
-        for h in hs:
-            h.wait_send()
-
-    def sent(k, carry):
-        forward(0, k).wait_send()
-        forward(1, k).wait_send()
-        back(k).wait_send()
-        return carry
-
-    lax.fori_loop(1, NEXP, sent, 0)
-
-    def passed_on(k, carry):
-        wcopy(k, 1, w_s1).wait_send()
-        return carry
-
-    @pl.when((rel != 4) & (rel != 5))
-    def _():
-        lax.fori_loop(0, CHUNKS, passed_on, 0)
-
-    @pl.when(rel == 0)
-    def _():
-        def passed_down(k, carry):
-            wcopy(k, -1, w_s2).wait_send()
-            return carry
-
-        lax.fori_loop(0, CHUNKS, passed_down, 0)
-
-    cp_adv.wait()
-    cp_tend.wait()
+    for one in cp_tend:
+        one.wait()
 
 
 def copy_kernel(adv_in, tend_in, adv_out, tend_out, adv_v, tend_v, sem_in, sem_out):
@@ -580,7 +598,7 @@
         pltpu.VMEM((1, OUTW, HID), BF),
         pltpu.VMEM((SLOTS, FZ), BF),
         pltpu.VMEM((OUTW, SLOTS), BF),
-        dma((9,)),
+        dma((13,)),
         dma((16,)),
         dma((16,)),
         dma((CHUNKS,)),

time: 107 us -> 106 us (level)
  no operation moved by 1% of the time
where the time goes in v4:
time: 106 us
  Pallas kernels  105 us (99%)
    pallas_call x1, Pallas kernels, on_device(): pl.pallas_call(kernel, out_shape=(jax.ShapeDtypeStruct((F, LAT, LON), BF)...  102 us
    pallas_call x1, Pallas kernels, on_device(): pl.pallas_call(copy_kernel, out_shape=(jax.ShapeDtypeStruct(adv.shape, BF...  3.06 us

profile of v4, /device:TPU:1, one launch (start us, length us, event | category | flops | bytes accessed | tf_op | source)
XLA Modules:
  0.0 105.6 jit_solution(7316574557321325161)
XLA Ops:
  0.6 101.9 %step.1 = (bf16[556,16,128]{2,1,0:T(8,128)(2,1)}, bf16[16,368,128]{2,1,0:T(8,128)(2,1)}) custom-call(s32[16]{0:T(128)} %counts_hbm.1, s32[16,128]{1,0:T(8,128)} %bitcast.8, bf16[556,16,128]{2,1,0:T(8,128)(2,1)} %bitcast.6, bf16[16,2,128]{2,1,0:T(2,128)(2,1)} %bitcast.9, bf16[1,556,512]{2,1,0:T(8,128)(2,1)} %win_hbm.1, bf16[1,3,512,512]{3,2,1,0:T(8,128)(2,1)} %wmid_hbm.1, ...), custom_call_target="tpu_custom_call" | custom-call | tf_op jit(solution)/shard_map/step/pallas_call | solution.py:614
  102.5 3.1 %hand_over.1 = (bf16[556,16,128]{2,1,0:T(8,128)(2,1)}, bf16[16,368,128]{2,1,0:T(8,128)(2,1)}) custom-call(bf16[556,16,128]{2,1,0:T(8,128)(2,1)} %get-tuple-element.6.adv_in, bf16[16,368,128]{2,1,0:T(8,128)(2,1)} %get-tuple-element.7.tend_in), custom_call_target="tpu_custom_call" | custom-call | tf_op jit(solution)/shard_map/hand_over/pallas_call | solution.py:636

commit v5 on v4

--- a/solution.py
+++ b/solution.py
@@ -573,7 +573,7 @@
         pltpu.VMEM((LAT, LON), jnp.int32),
         pltpu.VMEM((LAT, OUTW, LON), BF),
         pltpu.VMEM((F, LAT, LON), BF),
-        pltpu.VMEM((FP * LAT, LON), F32),
+        pltpu.VMEM(((FP + 1) * LAT, LON), F32),
         pltpu.VMEM((LAT, FP, LON), BF),
         pltpu.VMEM((LAT, FP, LON), BF),
         pltpu.VMEM((LAT, FZ, LON), BF),

time: 106 us -> 106 us (level)
  no operation moved by 1% of the time
where the time goes in v5:
time: 106 us
  Pallas kernels  105 us (99%)
    pallas_call x1, Pallas kernels, on_device(): pl.pallas_call(kernel, out_shape=(jax.ShapeDtypeStruct((F, LAT, LON), BF)...  102 us
    pallas_call x1, Pallas kernels, on_device(): pl.pallas_call(copy_kernel, out_shape=(jax.ShapeDtypeStruct(adv.shape, BF...  3.06 us

profile of v5, /device:TPU:1, one launch (start us, length us, event | category | flops | bytes accessed | tf_op | source)
XLA Modules:
  0.0 105.6 jit_solution(9010867539028348559)
XLA Ops:
  0.6 101.9 %step.1 = (bf16[556,16,128]{2,1,0:T(8,128)(2,1)}, bf16[16,368,128]{2,1,0:T(8,128)(2,1)}) custom-call(s32[16]{0:T(128)} %counts_hbm.1, s32[16,128]{1,0:T(8,128)} %bitcast.8, bf16[556,16,128]{2,1,0:T(8,128)(2,1)} %bitcast.6, bf16[16,2,128]{2,1,0:T(2,128)(2,1)} %bitcast.9, bf16[1,556,512]{2,1,0:T(8,128)(2,1)} %win_hbm.1, bf16[1,3,512,512]{3,2,1,0:T(8,128)(2,1)} %wmid_hbm.1, ...), custom_call_target="tpu_custom_call" | custom-call | tf_op jit(solution)/shard_map/step/pallas_call | solution.py:614
  102.6 3.1 %hand_over.1 = (bf16[556,16,128]{2,1,0:T(8,128)(2,1)}, bf16[16,368,128]{2,1,0:T(8,128)(2,1)}) custom-call(bf16[556,16,128]{2,1,0:T(8,128)(2,1)} %get-tuple-element.6.adv_in, bf16[16,368,128]{2,1,0:T(8,128)(2,1)} %get-tuple-element.7.tend_in), custom_call_target="tpu_custom_call" | custom-call | tf_op jit(solution)/shard_map/hand_over/pallas_call | solution.py:636
